TPU v7x, 256 devices: a whole 4x4x8 slice. The times are simulated.
256 devices in a mesh: row: 4 (over y), col: 16 (over z, core), layer: 4 (over x).
Axes of the slice: x: 4, y: 4, z: 8, core: 2. Of those that a mesh axis runs over, the one named last changes fastest.
Arguments:
- matrix: float32 [8192, 8192], P('row', ('layer', 'col')), may hold values from -1 to 1, as said below
- pattern: int32 [64, 64], P('row', ('layer', 'col')), may hold values from 0 to 1, as said below
Outputs:
- product: float32 [8192, 8192], P('row', ('col', 'layer'))
Inputs may be any that keep to these rules, and one draw needn't show every extreme that they name: symmetric: matrix[a, b] equals matrix[b, a]. `pattern`: symmetric; in each of the 4 aligned bands of 16 block columns every block row holds exactly 7 ones, and every diagonal entry is 1.
All inputs are finite; a program needn't handle non-finite values.
Results may differ from a plain program's by a relative error of at most 0.00007.
Values sent between devices are 32-bit elements; how exact they have to be, the bound alone decides.
A program may use at most 128 MiB of HBM per device.

v0:
```python
import jax
import jax.numpy as jnp
from jax import lax
from jax.sharding import PartitionSpec as P

PER_BAND = 7


def shards(matrix, pattern):
    rows_tile, cols_tile = pattern.shape
    block_size = matrix.shape[0] // rows_tile
    occupied_flag = pattern.astype(jnp.float32)
    masked = (
        matrix.reshape(rows_tile, block_size, cols_tile, block_size)
        * occupied_flag[:, None, :, None]
    ).reshape(matrix.shape)
    row_panel = lax.all_gather(masked, "col", axis=1, tiled=True)
    band_blocks = row_panel.shape[1] // block_size
    block_rows = rows_tile * lax.axis_size("row")
    strip_rows = block_rows // lax.axis_size("col")
    take_rows = min(strip_rows, rows_tile)
    sources = max(1, strip_rows // rows_tile)
    first_row = lax.axis_index("col") * strip_rows
    own_start = lax.axis_index("row") * rows_tile
    offset = jnp.clip(first_row - own_start, 0, rows_tile - take_rows)
    owner_row = first_row // rows_tile
    mirror_count = sources * take_rows
    band_pattern = lax.all_gather(pattern, "col", axis=1, tiled=True)
    all_pattern = lax.all_gather(band_pattern, "row", axis=0, tiled=True)
    piece_flags = lax.dynamic_slice_in_dim(band_pattern, offset, take_rows, 0)
    piece_index = jnp.argsort(1 - piece_flags, axis=1, stable=True)[:, :PER_BAND]
    panel_blocks = row_panel.reshape(rows_tile, block_size, band_blocks, block_size).transpose(
        0, 2, 1, 3
    )
    piece_blocks = lax.dynamic_slice_in_dim(panel_blocks, offset, take_rows, 0)
    packed = jnp.take_along_axis(piece_blocks, piece_index[:, :, None, None], axis=1)
    gathered = lax.all_gather(packed, "row", axis=0, tiled=True)
    mirror_packed = lax.dynamic_slice_in_dim(gathered, owner_row * take_rows, mirror_count, 0)
    mirror_flags = lax.dynamic_slice_in_dim(all_pattern, first_row, mirror_count, 0)
    mirror_index = jnp.argsort(1 - mirror_flags, axis=1, stable=True)[:, :PER_BAND]

    def one_column(operands):
        chosen_index, chosen_blocks = operands
        selected = jnp.take(panel_blocks, chosen_index, axis=1)
        return jnp.einsum(
            "iskl,sml->ikm",
            selected,
            chosen_blocks,
            precision=lax.Precision.HIGHEST,
            preferred_element_type=jnp.float32,
        )

    columns = lax.map(one_column, (mirror_index, mirror_packed))
    partial_value = columns.transpose(1, 2, 0, 3).reshape(
        rows_tile * block_size, mirror_count * block_size
    )
    return lax.psum_scatter(partial_value, "layer", scatter_dimension=1, tiled=True)


def solution(mesh):
    return jax.shard_map(
        shards,
        mesh=mesh,
        in_specs=(P("row", ("layer", "col")), P("row", ("layer", "col"))),
        out_specs=P("row", ("col", "layer")),
        check_vma=False,
    )
```

profile of v0, /device:TPU:17, one launch (start us, length us, event | category | flops | bytes accessed | tf_op | source)
XLA Modules:
  0.0 356.6 jit_solution(3417613894275846604)
XLA Ops:
  7.3 2.5 broadcast_multiply_fusion
  9.9 20.5 %all-gather = s32[16,1,16]{2,1,0:T(1,128)S(1)} all-gather(s32[1,1,16]{2,1,0:T(1,128)} %bitcast.78), channel_id=1, replica_groups=mesh['row'=4,'col'=16,'layer'=4] {'col'}, dimensions={0}, use_global_device_ids=true | all-gather | bytes 1088 | tf_op jit(solution)/shard_map/all_gather | solution.py:28
  31.7 84.4 %all-gather.4.cloned.1.call-done = f32[2048,2048]{1,0:T(8,128)} async-done(((f32[2048,128]{1,0:T(8,128)}), f32[2048,2048]{1,0:T(8,128)}) %all-gather.4.cloned.1.call-update) | async-done | bytes 16777232 | tf_op jit(solution)/shard_map/all_gather | solution.py:17
  116.1 9.4 %copy.49 = f32[256,8,16,128]{3,2,1,0:T(8,128)S(1)} copy(f32[256,8,16,128]{3,1,2,0:T(8,128)} %bitcast.70) | data formatting | bytes 33554432
  125.5 5.7 %copy-done = f32[256,8,16,128]{3,2,1,0:T(8,128)} copy-done((f32[256,8,16,128]{3,2,1,0:T(8,128)}, f32[256,8,16,128]{3,2,1,0:T(8,128)S(1)}, u32[]{:S(2)}) %copy-start) | copy-done | bytes 16777240
  131.6 3.2 copy.54
  134.8 2.9 gather_fusion.1
  139.3 8.2 %all_gather.13 = s32[64,16]{1,0:T(8,128)S(1)} all-gather(s32[16,16]{1,0:T(8,128)S(1)} %copy.35), channel_id=1, replica_groups=mesh['row'=4,'col'=16,'layer'=4] {'row'}, dimensions={0}, use_global_device_ids=true | all-gather | bytes 5120 | tf_op jit(solution)/shard_map/all_gather | solution.py:29
  148.5 8.2 %bitcast_bitcast_fusion = f32[16,16,128,128]{3,1,2,0:T(8,128)S(1)} fusion(f32[16,128,16,128]{3,2,1,0:T(8,128)} %bitcast.69), kind=kLoop, calls=%fused_computation.35 | loop fusion | bytes 33554432 | tf_op jit(solution)/shard_map/transpose | solution.py:32
  156.7 7.9 %copy.43 = f32[16,16,128,128]{3,2,1,0:T(8,128)} copy(f32[16,16,128,128]{3,1,2,0:T(8,128)S(1)} %bitcast_bitcast_fusion) | data formatting | bytes 33554432 | tf_op jit(solution)/shard_map/while | solution.py:53
  164.6 49.9 %all-gather.6.cloned.1.call-done = f32[16,7,128,128]{3,2,1,0:T(8,128)} async-done(((f32[4,7,128,128]{3,2,1,0:T(8,128)}), f32[16,7,128,128]{3,2,1,0:T(8,128)}) %all-gather.6.cloned.1.call-update) | async-done | bytes 7340048 | tf_op jit(solution)/shard_map/all_gather | solution.py:37
  214.4 1.6 constant_dynamic-slice_fusion.1
  216.1 75.8 %while.10 = (s32[]{:T(128)}, f32[4,16,128,128]{3,2,1,0:T(8,128)}, s32[4,7]{1,0:T(4,128)S(1)}, f32[16,16,128,128]{3,2,1,0:T(8,128)}, f32[4,7,128,128]{3,2,1,0:T(8,128)S(1)}, /*index=5*/s32[]{:T(128)}) while((s32[]{:T(128)}, f32[4,16,128,128]{3,2,1,0:T(8,128)}, s32[4,7]{1,0:T(4,128)S(1)}, f32[16,16,128,128]{3,2,1,0:T(8,128)}, ...), condition=%wide.region_3.4_spmd, body=%wide.region_2.3_spmd.sunk | while | flops 2820408320 | bytes 23533280 | solution.py:53
  216.1 9.8 %gather_fusion = f32[7,16,128,128]{3,2,1,0:T(8,128)} fusion(f32[16,16,128,128]{3,2,1,0:T(8,128)} %get-tuple-element.113, s32[1024]{0:T(1024)S(1)} %pad_clamp_fusion.2), kind=kCustom, calls=%fused_computation.clone.1 | custom fusion | bytes 14680092 | tf_op jit(solution)/shard_map/while/body/eval_jaxpr/jit(_take)/gather | solution.py:44
  225.9 9.2 %fusion.23 = f32[4,16,128,128]{3,2,1,0:T(8,128)} fusion(f32[4,16,128,128]{3,2,1,0:T(8,128)} %get-tuple-element.105, s32[]{:T(128)} %get-tuple-element.104, f32[7,16,128,128]{3,2,1,0:T(8,128)} %gather_fusion, pred[7]{0:T(512)(128)(4,1)S(1)} %compare_and_fusion.3, f32[4,7,128,128]{3,2,1,0:T(8,128)S(1)} %get-tuple-element.114), kind=kOutput, calls=%fused_computation.8.clone.1 | convolution fusion | flops 2820407296 | bytes 8848896 | tf_op jit(solution)/shard_map/while/body/eval_jaxpr/iskl,sml->ikm/dot_general | solution.py:45
  235.1 9.8 %gather_fusion = f32[7,16,128,128]{3,2,1,0:T(8,128)} fusion(f32[16,16,128,128]{3,2,1,0:T(8,128)} %get-tuple-element.113, s32[1024]{0:T(1024)S(1)} %pad_clamp_fusion.2), kind=kCustom, calls=%fused_computation.clone.1 | custom fusion | bytes 14680092 | tf_op jit(solution)/shard_map/while/body/eval_jaxpr/jit(_take)/gather | solution.py:44
  244.8 9.2 %fusion.23 = f32[4,16,128,128]{3,2,1,0:T(8,128)} fusion(f32[4,16,128,128]{3,2,1,0:T(8,128)} %get-tuple-element.105, s32[]{:T(128)} %get-tuple-element.104, f32[7,16,128,128]{3,2,1,0:T(8,128)} %gather_fusion, pred[7]{0:T(512)(128)(4,1)S(1)} %compare_and_fusion.3, f32[4,7,128,128]{3,2,1,0:T(8,128)S(1)} %get-tuple-element.114), kind=kOutput, calls=%fused_computation.8.clone.1 | convolution fusion | flops 2820407296 | bytes 8848896 | tf_op jit(solution)/shard_map/while/body/eval_jaxpr/iskl,sml->ikm/dot_general | solution.py:45
  254.0 9.8 %gather_fusion = f32[7,16,128,128]{3,2,1,0:T(8,128)} fusion(f32[16,16,128,128]{3,2,1,0:T(8,128)} %get-tuple-element.113, s32[1024]{0:T(1024)S(1)} %pad_clamp_fusion.2), kind=kCustom, calls=%fused_computation.clone.1 | custom fusion | bytes 14680092 | tf_op jit(solution)/shard_map/while/body/eval_jaxpr/jit(_take)/gather | solution.py:44
  263.8 9.1 %fusion.23 = f32[4,16,128,128]{3,2,1,0:T(8,128)} fusion(f32[4,16,128,128]{3,2,1,0:T(8,128)} %get-tuple-element.105, s32[]{:T(128)} %get-tuple-element.104, f32[7,16,128,128]{3,2,1,0:T(8,128)} %gather_fusion, pred[7]{0:T(512)(128)(4,1)S(1)} %compare_and_fusion.3, f32[4,7,128,128]{3,2,1,0:T(8,128)S(1)} %get-tuple-element.114), kind=kOutput, calls=%fused_computation.8.clone.1 | convolution fusion | flops 2820407296 | bytes 8848896 | tf_op jit(solution)/shard_map/while/body/eval_jaxpr/iskl,sml->ikm/dot_general | solution.py:45
  273.0 9.8 %gather_fusion = f32[7,16,128,128]{3,2,1,0:T(8,128)} fusion(f32[16,16,128,128]{3,2,1,0:T(8,128)} %get-tuple-element.113, s32[1024]{0:T(1024)S(1)} %pad_clamp_fusion.2), kind=kCustom, calls=%fused_computation.clone.1 | custom fusion | bytes 14680092 | tf_op jit(solution)/shard_map/while/body/eval_jaxpr/jit(_take)/gather | solution.py:44
  282.7 9.1 %fusion.23 = f32[4,16,128,128]{3,2,1,0:T(8,128)} fusion(f32[4,16,128,128]{3,2,1,0:T(8,128)} %get-tuple-element.105, s32[]{:T(128)} %get-tuple-element.104, f32[7,16,128,128]{3,2,1,0:T(8,128)} %gather_fusion, pred[7]{0:T(512)(128)(4,1)S(1)} %compare_and_fusion.3, f32[4,7,128,128]{3,2,1,0:T(8,128)S(1)} %get-tuple-element.114), kind=kOutput, calls=%fused_computation.8.clone.1 | convolution fusion | flops 2820407296 | bytes 8848896 | tf_op jit(solution)/shard_map/while/body/eval_jaxpr/iskl,sml->ikm/dot_general | solution.py:45
  291.9 5.0 %copy.44 = f32[16,128,4,128]{3,2,1,0:T(4,128)S(1)} copy(f32[16,128,4,128]{3,1,0,2:T(8,128)} %bitcast.75) | data formatting | bytes 8388608 | tf_op jit(solution)/shard_map/transpose | solution.py:54
  296.9 2.4 copy.53
  299.2 50.8 %reduce-scatter.2.cloned.1.call-done = f32[2048,128]{1,0:T(8,128)} async-done(((f32[2048,512]{1,0:T(8,128)}), f32[2048,128]{1,0:T(8,128)}) %reduce-scatter.2.cloned.1.call-update) | async-done | bytes 1048592 | tf_op jit(solution)/shard_map/reduce_scatter | solution.py:57
  (44 shorter events, 5.1 us)
Async XLA Ops:
  6.5 109.6 %all-gather.4.cloned.1.call-start = ((), (), s32[]{:S(2)}) async-start(), calls=%async_computation.1 | async-start | bytes 17825792 | tf_op jit(solution)/shard_map/all_gather | solution.py:17
  9.8 204.6 %all-gather.6.cloned.1.call-start = ((), (), s32[]{:S(2)}) async-start(), calls=%async_computation.2 | async-start | bytes 9175040 | tf_op jit(solution)/shard_map/all_gather | solution.py:37
  125.5 5.7 %copy-start = (f32[256,8,16,128]{3,2,1,0:T(8,128)}, f32[256,8,16,128]{3,2,1,0:T(8,128)S(1)}, u32[]{:S(2)}) copy-start(f32[256,8,16,128]{3,2,1,0:T(8,128)S(1)} %copy.49) | copy-start | bytes 50331652
  139.2 210.9 %reduce-scatter.2.cloned.1.call-start = ((), (), s32[]{:S(2)}) async-start(), calls=%async_computation.3 | async-start | bytes 5242880 | tf_op jit(solution)/shard_map/reduce_scatter | solution.py:57
Sparse Core Ops, SparseCore 0:
  9.9 106.1 all-gather.3
  139.3 75.0 all-gather.5
  299.4 50.6 reduce-scatter.1
where the time goes:
time: 358 us; the launch traced here: 357 us
  waiting for transfers between devices  185 us (52%)
  local copies, waits for them, and re-layouts  86.5 us (24%)
  matrix products  36.6 us (10%)
  blocking collectives  28.8 us (8%)
  between operations  13.2 us (4%)
  other arithmetic  6.24 us (2%)
    all_gather x1, waiting for transfers between devices, shards(): row_panel = lax.all_gather(masked, 'col', axis=1, tiled=True)  84.4 us
    reduce_scatter x1, waiting for transfers between devices, shards(): lax.psum_scatter(partial_value, 'layer', scatter_dimension=1, tiled=True)  50.8 us
    all_gather x1, waiting for transfers between devices, shards(): gathered = lax.all_gather(packed, 'row', axis=0, tiled=True)  49.9 us
    gather x4, local copies, waits for them, and re-layouts, one_column(): selected = jnp.take(panel_blocks, chosen_index, axis=1)  39 us
    dot_general x4, matrix products, one_column(): jnp.einsum('iskl,sml->ikm', selected, chosen_blocks, precision=lax.Precis...  36.6 us
    unnamed x9, local copies, waits for them, and re-layouts  21 us
    all_gather x1, blocking collectives, shards(): band_pattern = lax.all_gather(pattern, 'col', axis=1, tiled=True)  20.5 us
    all_gather x1, blocking collectives, shards(): all_pattern = lax.all_gather(band_pattern, 'row', axis=0, tiled=True)  8.25 us
  transfers between devices with their start and end apart: 3, of which 3 were waited for; matrix products, arithmetic and copies ran while one was open for 5% of the time, Pallas kernels for 0%

commit v1 on v0

v1 whole, which is shorter than its diff:
```python
import functools

import jax
import jax.numpy as jnp
from jax import lax
from jax.experimental import pallas as pl
from jax.experimental.pallas import tpu as pltpu
from jax.sharding import PartitionSpec as P

BS = 128
PER = 7
BAND = 16
UNITS = 8
LIST, SLOT, FLAG = 0, 1, 2


def index_tile(pattern):
    flags = pattern[:, 0]
    place = lax.broadcasted_iota(jnp.int32, (BAND, BAND), 0)
    upto = lax.broadcasted_iota(jnp.int32, (BAND, BAND), 1)
    count = jnp.sum(jnp.where(place <= upto, flags[:, None], 0), axis=0)
    order = lax.broadcasted_iota(jnp.int32, (BAND, BAND), 1)
    listed = jnp.sum((count[:, None] <= order).astype(jnp.int32), axis=0)
    rows = jnp.stack([jnp.minimum(listed, BAND - 1), jnp.clip(count - 1, 0, PER - 1), flags])
    return jnp.pad(rows, ((0, 8 - 3), (0, 128 - BAND)))


def split(value):
    high = value.astype(jnp.bfloat16)
    low = (value - high.astype(jnp.float32)).astype(jnp.bfloat16)
    return jnp.concatenate([high, low], axis=1)


def kernel(
    mat, meta_s, meta_v, out,
    packed_a, packed_b, a_units, a_meta, a_idx, b_meta, b_idx, b_dense, weights,
    partial, merged, opposite, from_left, from_right, from_twin,
    a_send, a_recv, am_send, am_recv, b_send, b_recv, bm_send, bm_recv, idx_sem,
    opp_send, opp_recv, mg_send, un_send, left_recv, right_recv, twin_send, twin_recv,
    *b_units,
):
    y, col, x = lax.axis_index("row"), lax.axis_index("col"), lax.axis_index("layer")
    z, q = col // 2, col % 2
    turn = 1 - 2 * q

    def at(row=None, col_=None, layer=None):
        return {
            "row": y if row is None else row,
            "col": col if col_ is None else col_,
            "layer": x if layer is None else layer,
        }

    def zdev(step):
        return at(col_=2 * ((z + step + 8) % 8) + q)

    def ydev(step):
        return at(row=(y + step + 4) % 4)

    def xdev(step, core):
        return at(col_=2 * z + core, layer=(x + step + 4) % 4)

    twin = at(col_=2 * z + 1 - q)
    a_partner = at(row=x, layer=y)
    a_self = x == y
    b_target = at(row=(col % 8) // 2, col_=2 * (2 * x + col // 8) + col % 2, layer=y)
    b_source = at(row=x, col_=8 * (z % 2) + 2 * y + q, layer=z // 2)
    b_self = (y == x) & ((col % 8) // 2 == y) & (2 * (2 * x + col // 8) + col % 2 == col)

    barrier = pltpu.get_barrier_semaphore()

    def greet(device):
        pl.semaphore_signal(barrier, inc=1, device_id=device, device_id_type=pl.DeviceIdType.MESH)

    for device in (
        zdev(1), zdev(-1), ydev(1), ydev(-1), twin,
        xdev(1, 0), xdev(1, 1), xdev(-1, 0), xdev(-1, 1),
    ):
        greet(device)

    @pl.when(jnp.logical_not(a_self))
    def _():
        greet(a_partner)

    @pl.when(jnp.logical_not(b_self))
    def _():
        greet(b_source)

    for s in range(PER):
        block = mat[meta_s[LIST, s]]
        packed_a[s] = block
        packed_b[s] = block.T

    expected = 11 - a_self.astype(jnp.int32) - b_self.astype(jnp.int32)
    pl.semaphore_wait(barrier, expected)

    def remote(src, dst, send, recv, device):
        return pltpu.make_async_remote_copy(
            src_ref=src, dst_ref=dst, send_sem=send, recv_sem=recv,
            device_id=device, device_id_type=pl.DeviceIdType.MESH,
        )

    def got(dst, send, recv):
        remote(dst, dst, send, recv, twin).wait_recv()

    def sent(src, send, recv):
        remote(src, src, send, recv, twin).wait_send()

    def send_a(t, data, meta, device):
        remote(meta, a_meta.at[t], am_send.at[t], am_recv.at[t], device).start()
        remote(data, a_units.at[t], a_send.at[t], a_recv.at[t], device).start()

    def send_b(u, data, meta, device):
        remote(meta, b_meta.at[u], bm_send.at[u], bm_recv.at[u], device).start()
        remote(data, b_units[u], b_send.at[u], b_recv.at[u], device).start()

    @pl.when(jnp.logical_not(b_self))
    def _():
        send_b(0, packed_b, meta_v, b_target)

    @pl.when(b_self)
    def _():
        pltpu.make_async_copy(meta_v, b_meta.at[0], bm_recv.at[0]).start()
        pltpu.make_async_copy(packed_b, b_units[0], b_recv.at[0]).start()

    @pl.when(jnp.logical_not(a_self))
    def _():
        send_a(0, packed_a, meta_v, a_partner)

    @pl.when(a_self)
    def _():
        pltpu.make_async_copy(meta_v, a_meta.at[0], am_recv.at[0]).start()
        pltpu.make_async_copy(packed_a, a_units.at[0], a_recv.at[0]).start()

    def a_arrive(t):
        got(a_meta.at[t], am_send.at[t], am_recv.at[t])
        index = pltpu.make_async_copy(a_meta.at[t], a_idx.at[t], idx_sem)
        index.start()
        got(a_units.at[t], a_send.at[t], a_recv.at[t])
        index.wait()

    def a_forward(t):
        way = jnp.where(t % 2 == 1, turn, -turn)
        send_a(t + 2, a_units.at[t], a_meta.at[t], zdev(way))

    def b_arrive(u):
        got(b_meta.at[u], bm_send.at[u], bm_recv.at[u])
        index = pltpu.make_async_copy(b_meta.at[u], b_idx.at[u], idx_sem)
        index.start()
        got(b_units[u], b_send.at[u], b_recv.at[u])
        index.wait()

    def b_unpack(u):
        way, core = (turn, q) if u < 4 else (-turn, 1 - q)
        unit = 2 * ((y + way * (0, -1, 1, -2)[u % 4] + 4) % 4) + core
        group, half = unit % 4, unit // 4

        def place(j, carry):
            block = b_units[u][b_idx[u, SLOT, j]] * b_idx[u, FLAG, j].astype(jnp.float32)
            b_dense[group, j, half] = split(block)
            return carry

        lax.fori_loop(0, BAND, place, 0)

    def b_twin(u):
        send_b(4 + u, b_units[u], b_meta.at[u], twin)

    a_arrive(0)
    send_a(1, a_units.at[0], a_meta.at[0], zdev(turn))
    send_a(2, a_units.at[0], a_meta.at[0], zdev(-turn))

    b_arrive(0)
    send_b(1, b_units[0], b_meta.at[0], ydev(turn))
    send_b(2, b_units[0], b_meta.at[0], ydev(-turn))
    b_twin(0)
    b_unpack(0)
    b_arrive(4)
    b_unpack(4)
    b_arrive(1)
    send_b(3, b_units[1], b_meta.at[1], ydev(turn))
    b_twin(1)
    b_arrive(2)
    b_twin(2)
    b_unpack(1)
    b_unpack(2)
    b_arrive(5)
    b_unpack(5)
    b_arrive(6)
    b_unpack(6)
    a_arrive(1)
    a_forward(1)
    a_arrive(2)
    a_forward(2)
    b_arrive(3)
    b_twin(3)
    b_unpack(3)
    b_arrive(7)
    b_unpack(7)

    def unit_row(t, way, core):
        step = jnp.where(t % 2 == 1, -((t + 1) // 2), t // 2)
        return 2 * ((z + way * step + 8) % 8) + core

    def merge(t):
        i = unit_row(t, turn, q)
        for h, j, step, box, sem in ((0, 1, 1, from_left, left_recv), (1, 2, -1, from_right, right_recv)):
            got(opposite.at[t, h], opp_send.at[t, h], opp_recv.at[t, h])
            merged[t, h] = opposite[t, h] + partial[t, j, h]
            remote(merged.at[t, h], box.at[i], mg_send.at[t, h], sem.at[i], xdev(step, h)).start()

    def finish(t):
        for core, way in ((q, turn), (1 - q, -turn)):
            i = unit_row(t, way, core)
            got(from_left.at[i], mg_send.at[0, 0], left_recv.at[i])
            got(from_right.at[i], mg_send.at[0, 0], right_recv.at[i])
            if core is q:
                own = partial[t, 3, q]
            else:
                got(from_twin.at[t], twin_send.at[t], twin_recv.at[t])
                own = from_twin[t]
            total = own + from_left[i] + from_right[i]
            out[pl.ds(pl.multiple_of(i * BS, BS), BS), :] = total.T

    def unit(t, carry):
        @pl.when(t >= 3)
        def _():
            a_arrive(t)

        @pl.when((t >= 3) & (t <= 5))
        def _():
            a_forward(t)

        for s in range(PER):
            part = split(a_units[t, s])
            weights[2 * s * BS : (2 * s + 1) * BS, :] = part
            weights[(2 * s + 1) * BS : (2 * s + 2) * BS, :] = part
        places = [a_idx[t, LIST, s] for s in range(PER)]
        i = unit_row(t, turn, q)
        for j, step in enumerate((2, 1, 3, 0)):
            group = (x + step) % 4
            left = jnp.concatenate(
                [b_dense[group, place].reshape(2 * BS, 2 * BS) for place in places], axis=1
            )
            both = jnp.dot(left, weights[...], preferred_element_type=jnp.float32)
            both = both[:, :BS] + both[:, BS:]
            partial[t, j, 0] = both[:BS]
            partial[t, j, 1] = both[BS:]
            if j == 0:
                for h, way in ((0, 1), (1, -1)):
                    remote(
                        partial.at[t, j, h], opposite.at[t, h], opp_send.at[t, h], opp_recv.at[t, h], xdev(way, q)
                    ).start()
            elif j == 1:
                remote(
                    partial.at[t, j, 1], from_left.at[i], un_send.at[t, 0], left_recv.at[i], xdev(1, 1)
                ).start()
            elif j == 2:
                remote(
                    partial.at[t, j, 0], from_right.at[i], un_send.at[t, 1], right_recv.at[i], xdev(-1, 0)
                ).start()
            else:
                remote(
                    partial.at[t, j, 1 - q], from_twin.at[t], twin_send.at[t], twin_recv.at[t], twin
                ).start()

        @pl.when(t >= 1)
        def _():
            merge(t - 1)

        @pl.when(t >= 3)
        def _():
            finish(t - 3)

        return carry

    lax.fori_loop(0, UNITS, unit, 0)
    merge(UNITS - 1)

    def last(t, carry):
        finish(t)
        return carry

    lax.fori_loop(UNITS - 3, UNITS, last, 0)

    @pl.when(jnp.logical_not(a_self))
    def _():
        sent(a_meta.at[0], am_send.at[0], am_recv.at[0])
        sent(a_units.at[0], a_send.at[0], a_recv.at[0])

    @pl.when(jnp.logical_not(b_self))
    def _():
        sent(b_meta.at[0], bm_send.at[0], bm_recv.at[0])
        sent(b_units[0], b_send.at[0], b_recv.at[0])

    for k in range(1, UNITS):
        sent(a_meta.at[k], am_send.at[k], am_recv.at[k])
        sent(a_units.at[k], a_send.at[k], a_recv.at[k])
        sent(b_meta.at[k], bm_send.at[k], bm_recv.at[k])
        sent(b_units[k], b_send.at[k], b_recv.at[k])

    def drain(t, carry):
        for h in range(2):
            sent(opposite.at[t, h], opp_send.at[t, h], opp_recv.at[t, h])
            sent(merged.at[t, h], mg_send.at[t, h], opp_recv.at[t, h])
            sent(merged.at[t, h], un_send.at[t, h], opp_recv.at[t, h])
        sent(from_twin.at[t], twin_send.at[t], twin_recv.at[t])
        return carry

    lax.fori_loop(0, UNITS, drain, 0)


def shards(matrix, pattern):
    f32, i32 = jnp.float32, jnp.int32
    meta = index_tile(pattern)
    dma = pltpu.SemaphoreType.DMA
    return pl.pallas_call(
        kernel,
        out_shape=jax.ShapeDtypeStruct(matrix.shape, f32),
        in_specs=[
            pl.BlockSpec(memory_space=pltpu.VMEM),
            pl.BlockSpec(memory_space=pltpu.SMEM),
            pl.BlockSpec(memory_space=pltpu.VMEM),
        ],
        out_specs=pl.BlockSpec(memory_space=pltpu.VMEM),
        scratch_shapes=[
            pltpu.VMEM((PER, BS, BS), f32),
            pltpu.VMEM((PER, BS, BS), f32),
            pltpu.VMEM((UNITS, PER, BS, BS), f32),
            pltpu.VMEM((UNITS, 8, 128), i32),
            pltpu.SMEM((UNITS, 8, 128), i32),
            pltpu.VMEM((UNITS, 8, 128), i32),
            pltpu.SMEM((UNITS, 8, 128), i32),
            pltpu.VMEM((4, BAND, 2, BS, 2 * BS), jnp.bfloat16),
            pltpu.VMEM((PER * 2 * BS, 2 * BS), jnp.bfloat16),
            pltpu.VMEM((UNITS, 4, 2, BS, BS), f32),
            pltpu.VMEM((UNITS, 2, BS, BS), f32),
            pltpu.VMEM((UNITS, 2, BS, BS), f32),
            pltpu.VMEM((BAND, BS, BS), f32),
            pltpu.VMEM((BAND, BS, BS), f32),
            pltpu.VMEM((UNITS, BS, BS), f32),
        ]
        + [dma((UNITS,))] * 8
        + [dma]
        + [dma((UNITS, 2))] * 4
        + [dma((BAND,))] * 2
        + [dma((UNITS,))] * 2
        + [pltpu.VMEM((PER, BS, BS), f32)] * UNITS,
        compiler_params=pltpu.CompilerParams(
            collective_id=0, has_side_effects=True, vmem_limit_bytes=52 * 1024 * 1024
        ),
    )(matrix.reshape(BAND, BS, BS), meta, meta)


def solution(mesh):
    return jax.shard_map(
        shards,
        mesh=mesh,
        in_specs=(P("row", ("layer", "col")), P("row", ("layer", "col"))),
        out_specs=P("row", ("col", "layer")),
        check_vma=False,
    )
```

time: 358 us -> 133 us (0.37)
  waiting for transfers between devices: 185 us -> 0 us
  Pallas kernels: 0 us -> 129 us
  local copies, waits for them, and re-layouts: 86.5 us -> 1.63 us
  matrix products: 36.6 us -> 0 us
  blocking collectives: 28.8 us -> 0 us
  between operations: 13.2 us -> 0.02 us
  other arithmetic: 6.24 us -> 0.2 us
    all_gather x2 -> x0, waiting for transfers between devices: 134 us -> none  [the longest x1 84.4 us: shards(): row_panel = lax.all_gather(masked, 'col', axis=1, tiled=True)]
    pallas_call x0 -> x1, Pallas kernels: none -> 129 us  [shards(): pl.pallas_call(kernel, out_shape=jax.ShapeDtypeStruct(matrix.shape, f32),...]
    reduce_scatter x1 -> x0, waiting for transfers between devices: 50.8 us -> none  [shards(): lax.psum_scatter(partial_value, 'layer', scatter_dimension=1, tiled=True)]
    gather x7 -> x0, local copies, waits for them, and re-layouts: 42.1 us -> none  [the longest x4 39 us: one_column(): selected = jnp.take(panel_blocks, chosen_index, axis=1)]
    dot_general x4 -> x0, matrix products: 36.6 us -> none  [one_column(): jnp.einsum('iskl,sml->ikm', selected, chosen_blocks, precision=lax.Precis...]
    all_gather x2 -> x0, blocking collectives: 28.8 us -> none  [the longest x1 20.5 us: shards(): band_pattern = lax.all_gather(pattern, 'col', axis=1, tiled=True)]
    unnamed x9 -> x3, local copies, waits for them, and re-layouts: 21 us -> 1.63 us
    transpose x2 -> x0, local copies, waits for them, and re-layouts: 13.2 us -> none  [the longest x1 8.22 us: shards(): row_panel.reshape(rows_tile, block_size, band_blocks, block_size)]
  transfers between devices with their start and end apart: 3 -> 0, of which waited for: 3 -> 0; matrix products, arithmetic and copies ran while one was open for 5% -> 0% of each run, Pallas kernels for 0% -> 0%
where the time goes in v1:
time: 133 us; the launch traced here: 131 us
  Pallas kernels  129 us (97%)
  local copies, waits for them, and re-layouts  1.63 us (1%)
    pallas_call x1, Pallas kernels, shards(): pl.pallas_call(kernel, out_shape=jax.ShapeDtypeStruct(matrix.shape, f32),...  129 us

profile of v1, /device:TPU:17, one launch (start us, length us, event | category | flops | bytes accessed | tf_op | source)
XLA Modules:
  0.0 131.0 jit_solution(16623255651303016184)
XLA Ops:
  0.0 0.0 copy-start
  0.0 0.7 copy-done
  0.7 0.1 select_reduce_fusion
  0.7 0.1 convert_reduce_fusion
  0.9 129.1 %shard_map.28 = f32[2048,128]{1,0:T(8,128)S(1)} custom-call(f32[16,128,128]{2,1,0:T(8,128)} %bitcast.7, s32[8,128]{1,0:T(8,128)S(1)} %pad.4.meta_s.meta_v, s32[8,128]{1,0:T(8,128)S(1)} %pad.4.meta_s.meta_v), custom_call_target="tpu_custom_call" | custom-call | tf_op jit(solution)/shard_map/pallas_call | solution.py:315
  130.0 1.0 copy.4
  (3 shorter events, 0.0 us)
Async XLA Ops:
  0.0 0.7 copy-start

commit v2 on v1

--- a/solution.py
+++ b/solution.py
@@ -33,10 +33,11 @@
 
 def kernel(
     mat, meta_s, meta_v, out,
-    packed_a, packed_b, a_units, a_meta, a_idx, b_meta, b_idx, b_dense, weights,
-    partial, merged, opposite, from_left, from_right, from_twin,
+    packed, a_units, a_meta, a_idx, b_meta, b_idx, b_dense, weights,
+    partial, merged, opposite, from_left, from_right, from_twin, done, passing,
     a_send, a_recv, am_send, am_recv, b_send, b_recv, bm_send, bm_recv, idx_sem,
     opp_send, opp_recv, mg_send, un_send, left_recv, right_recv, twin_send, twin_recv,
+    done_send, pass_send, pass_recv, out_recv,
     *b_units,
 ):
     y, col, x = lax.axis_index("row"), lax.axis_index("col"), lax.axis_index("layer")
@@ -53,45 +54,37 @@
     def zdev(step):
         return at(col_=2 * ((z + step + 8) % 8) + q)
 
-    def ydev(step):
-        return at(row=(y + step + 4) % 4)
-
-    def xdev(step, core):
-        return at(col_=2 * z + core, layer=(x + step + 4) % 4)
+    def xdev(step):
+        return at(layer=(x + step + 4) % 4)
+
+    def ydev(step, core):
+        return at(row=(y + step + 4) % 4, col_=2 * z + core)
 
     twin = at(col_=2 * z + 1 - q)
-    a_partner = at(row=x, layer=y)
-    a_self = x == y
-    b_target = at(row=(col % 8) // 2, col_=2 * (2 * x + col // 8) + col % 2, layer=y)
-    b_source = at(row=x, col_=8 * (z % 2) + 2 * y + q, layer=z // 2)
-    b_self = (y == x) & ((col % 8) // 2 == y) & (2 * (2 * x + col // 8) + col % 2 == col)
 
     barrier = pltpu.get_barrier_semaphore()
 
     def greet(device):
         pl.semaphore_signal(barrier, inc=1, device_id=device, device_id_type=pl.DeviceIdType.MESH)
 
-    for device in (
-        zdev(1), zdev(-1), ydev(1), ydev(-1), twin,
-        xdev(1, 0), xdev(1, 1), xdev(-1, 0), xdev(-1, 1),
-    ):
+    for device in (xdev(1), xdev(2), xdev(3), ydev(1, 0), ydev(1, 1), ydev(-1, 0), ydev(-1, 1)):
         greet(device)
 
-    @pl.when(jnp.logical_not(a_self))
-    def _():
-        greet(a_partner)
-
-    @pl.when(jnp.logical_not(b_self))
-    def _():
-        greet(b_source)
+    def greet_line(k, carry):
+        greet(at(col_=(col + k) % BAND))
+        return carry
+
+    lax.fori_loop(1, BAND, greet_line, 0)
 
     for s in range(PER):
         block = mat[meta_s[LIST, s]]
-        packed_a[s] = block
-        packed_b[s] = block.T
-
-    expected = 11 - a_self.astype(jnp.int32) - b_self.astype(jnp.int32)
-    pl.semaphore_wait(barrier, expected)
+        packed[s] = block
+        b_units[0][s] = block.T
+    own_idx = pltpu.make_async_copy(meta_v, a_idx.at[0], idx_sem)
+    own_idx.start()
+    own_idx.wait()
+
+    pl.semaphore_wait(barrier, 7 + BAND - 1)
 
     def remote(src, dst, send, recv, device):
         return pltpu.make_async_remote_copy(
@@ -112,24 +105,6 @@
     def send_b(u, data, meta, device):
         remote(meta, b_meta.at[u], bm_send.at[u], bm_recv.at[u], device).start()
         remote(data, b_units[u], b_send.at[u], b_recv.at[u], device).start()
-
-    @pl.when(jnp.logical_not(b_self))
-    def _():
-        send_b(0, packed_b, meta_v, b_target)
-
-    @pl.when(b_self)
-    def _():
-        pltpu.make_async_copy(meta_v, b_meta.at[0], bm_recv.at[0]).start()
-        pltpu.make_async_copy(packed_b, b_units[0], b_recv.at[0]).start()
-
-    @pl.when(jnp.logical_not(a_self))
-    def _():
-        send_a(0, packed_a, meta_v, a_partner)
-
-    @pl.when(a_self)
-    def _():
-        pltpu.make_async_copy(meta_v, a_meta.at[0], am_recv.at[0]).start()
-        pltpu.make_async_copy(packed_a, a_units.at[0], a_recv.at[0]).start()
 
     def a_arrive(t):
         got(a_meta.at[t], am_send.at[t], am_recv.at[t])
@@ -151,45 +126,42 @@
 
     def b_unpack(u):
         way, core = (turn, q) if u < 4 else (-turn, 1 - q)
-        unit = 2 * ((y + way * (0, -1, 1, -2)[u % 4] + 4) % 4) + core
-        group, half = unit % 4, unit // 4
+        group = (x + way * (0, -1, 1, -2)[u % 4] + 4) % 4
 
         def place(j, carry):
-            block = b_units[u][b_idx[u, SLOT, j]] * b_idx[u, FLAG, j].astype(jnp.float32)
-            b_dense[group, j, half] = split(block)
+            slot = a_idx[0, SLOT, j] if u == 0 else b_idx[u, SLOT, j]
+            flag = a_idx[0, FLAG, j] if u == 0 else b_idx[u, FLAG, j]
+            b_dense[group, j, core] = split(b_units[u][slot] * flag.astype(jnp.float32))
             return carry
 
         lax.fori_loop(0, BAND, place, 0)
 
     def b_twin(u):
-        send_b(4 + u, b_units[u], b_meta.at[u], twin)
-
-    a_arrive(0)
-    send_a(1, a_units.at[0], a_meta.at[0], zdev(turn))
-    send_a(2, a_units.at[0], a_meta.at[0], zdev(-turn))
-
-    b_arrive(0)
-    send_b(1, b_units[0], b_meta.at[0], ydev(turn))
-    send_b(2, b_units[0], b_meta.at[0], ydev(-turn))
+        send_b(4 + u, b_units[u], meta_v if u == 0 else b_meta.at[u], twin)
+
+    send_b(1, b_units[0], meta_v, xdev(turn))
+    send_b(2, b_units[0], meta_v, xdev(-turn))
+    send_a(1, packed, meta_v, zdev(turn))
+    send_a(2, packed, meta_v, zdev(-turn))
     b_twin(0)
     b_unpack(0)
     b_arrive(4)
     b_unpack(4)
     b_arrive(1)
-    send_b(3, b_units[1], b_meta.at[1], ydev(turn))
+    send_b(3, b_units[1], b_meta.at[1], xdev(turn))
     b_twin(1)
     b_arrive(2)
     b_twin(2)
+    a_arrive(1)
+    a_forward(1)
+    a_arrive(2)
+    a_forward(2)
     b_unpack(1)
     b_unpack(2)
     b_arrive(5)
     b_unpack(5)
     b_arrive(6)
     b_unpack(6)
-    a_arrive(1)
-    a_forward(1)
-    a_arrive(2)
-    a_forward(2)
     b_arrive(3)
     b_twin(3)
     b_unpack(3)
@@ -205,7 +177,33 @@
         for h, j, step, box, sem in ((0, 1, 1, from_left, left_recv), (1, 2, -1, from_right, right_recv)):
             got(opposite.at[t, h], opp_send.at[t, h], opp_recv.at[t, h])
             merged[t, h] = opposite[t, h] + partial[t, j, h]
-            remote(merged.at[t, h], box.at[i], mg_send.at[t, h], sem.at[i], xdev(step, h)).start()
+            remote(merged.at[t, h], box.at[i], mg_send.at[t, h], sem.at[i], ydev(step, h)).start()
+
+    def block_out(k):
+        return out.at[pl.ds(pl.multiple_of(k * BS, BS), BS), :]
+
+    def deliver(value, src, m, step, send):
+        owner = 4 * ((x + step) % 4) + m
+
+        @pl.when(owner == col)
+        def _():
+            block_out(col)[...] = value[...]
+
+        @pl.when(owner != col)
+        def _():
+            remote(src, block_out(col), send, out_recv.at[col], at(col_=owner)).start()
+
+    def relay(t):
+        for core, way in ((q, turn), (1 - q, -turn)):
+            i = unit_row(t, way, core)
+            m = i // 4
+
+            @pl.when(i % 4 == x)
+            def _():
+                for step in (1, 3, 2):
+                    box = passing.at[m, step - 1]
+                    got(box, done_send.at[i], pass_recv.at[m, step - 1])
+                    deliver(box, box, m, step, pass_send.at[m, step - 1])
 
     def finish(t):
         for core, way in ((q, turn), (1 - q, -turn)):
@@ -218,7 +216,18 @@
                 got(from_twin.at[t], twin_send.at[t], twin_recv.at[t])
                 own = from_twin[t]
             total = own + from_left[i] + from_right[i]
-            out[pl.ds(pl.multiple_of(i * BS, BS), BS), :] = total.T
+            done[i] = total
+            m, step = i // 4, (x - i + 16) % 4
+
+            @pl.when(step == 0)
+            def _():
+                deliver(done.at[i], done.at[i], m, 0, done_send.at[i])
+
+            @pl.when(step != 0)
+            def _():
+                remote(
+                    done.at[i], passing.at[m, step - 1], done_send.at[i], pass_recv.at[m, step - 1], at(layer=i % 4)
+                ).start()
 
     def unit(t, carry):
         @pl.when(t >= 3)
@@ -229,14 +238,24 @@
         def _():
             a_forward(t)
 
-        for s in range(PER):
-            part = split(a_units[t, s])
-            weights[2 * s * BS : (2 * s + 1) * BS, :] = part
-            weights[(2 * s + 1) * BS : (2 * s + 2) * BS, :] = part
+        def weigh(load):
+            for s in range(PER):
+                part = split(load(s))
+                weights[2 * s * BS : (2 * s + 1) * BS, :] = part
+                weights[(2 * s + 1) * BS : (2 * s + 2) * BS, :] = part
+
+        @pl.when(t == 0)
+        def _():
+            weigh(lambda s: packed[s])
+
+        @pl.when(t > 0)
+        def _():
+            weigh(lambda s: a_units[t, s])
+
         places = [a_idx[t, LIST, s] for s in range(PER)]
         i = unit_row(t, turn, q)
         for j, step in enumerate((2, 1, 3, 0)):
-            group = (x + step) % 4
+            group = (y + step) % 4
             left = jnp.concatenate(
                 [b_dense[group, place].reshape(2 * BS, 2 * BS) for place in places], axis=1
             )
@@ -247,15 +266,15 @@
             if j == 0:
                 for h, way in ((0, 1), (1, -1)):
                     remote(
-                        partial.at[t, j, h], opposite.at[t, h], opp_send.at[t, h], opp_recv.at[t, h], xdev(way, q)
+                        partial.at[t, j, h], opposite.at[t, h], opp_send.at[t, h], opp_recv.at[t, h], ydev(way, q)
                     ).start()
             elif j == 1:
                 remote(
-                    partial.at[t, j, 1], from_left.at[i], un_send.at[t, 0], left_recv.at[i], xdev(1, 1)
+                    partial.at[t, j, 1], from_left.at[i], un_send.at[t, 0], left_recv.at[i], ydev(1, 1)
                 ).start()
             elif j == 2:
                 remote(
-                    partial.at[t, j, 0], from_right.at[i], un_send.at[t, 1], right_recv.at[i], xdev(-1, 0)
+                    partial.at[t, j, 0], from_right.at[i], un_send.at[t, 1], right_recv.at[i], ydev(-1, 0)
                 ).start()
             else:
                 remote(
@@ -270,6 +289,10 @@
         def _():
             finish(t - 3)
 
+        @pl.when(t >= 4)
+        def _():
+            relay(t - 4)
+
         return carry
 
     lax.fori_loop(0, UNITS, unit, 0)
@@ -277,19 +300,12 @@
 
     def last(t, carry):
         finish(t)
+        relay(t - 1)
         return carry
 
     lax.fori_loop(UNITS - 3, UNITS, last, 0)
 
-    @pl.when(jnp.logical_not(a_self))
-    def _():
-        sent(a_meta.at[0], am_send.at[0], am_recv.at[0])
-        sent(a_units.at[0], a_send.at[0], a_recv.at[0])
-
-    @pl.when(jnp.logical_not(b_self))
-    def _():
-        sent(b_meta.at[0], bm_send.at[0], bm_recv.at[0])
-        sent(b_units[0], b_send.at[0], b_recv.at[0])
+    relay(UNITS - 1)
 
     for k in range(1, UNITS):
         sent(a_meta.at[k], am_send.at[k], am_recv.at[k])
@@ -306,6 +322,25 @@
         return carry
 
     lax.fori_loop(0, UNITS, drain, 0)
+
+    def collect(k, carry):
+        @pl.when((k % 4 != x) | (4 * x + k // 4 != col))
+        def _():
+            sent(done.at[k], done_send.at[k], out_recv.at[k])
+
+        @pl.when(k != col)
+        def _():
+            got(block_out(k), done_send.at[k], out_recv.at[k])
+
+        for step in (1, 2, 3):
+            @pl.when((k < 4) & (4 * ((x + step) % 4) + k != col))
+            def _():
+                m = lax.rem(k, 4)
+                sent(passing.at[m, step - 1], pass_send.at[m, step - 1], out_recv.at[k])
+
+        return carry
+
+    lax.fori_loop(0, BAND, collect, 0)
 
 
 def shards(matrix, pattern):
@@ -323,7 +358,6 @@
         out_specs=pl.BlockSpec(memory_space=pltpu.VMEM),
         scratch_shapes=[
             pltpu.VMEM((PER, BS, BS), f32),
-            pltpu.VMEM((PER, BS, BS), f32),
             pltpu.VMEM((UNITS, PER, BS, BS), f32),
             pltpu.VMEM((UNITS, 8, 128), i32),
             pltpu.SMEM((UNITS, 8, 128), i32),
@@ -337,12 +371,15 @@
             pltpu.VMEM((BAND, BS, BS), f32),
             pltpu.VMEM((BAND, BS, BS), f32),
             pltpu.VMEM((UNITS, BS, BS), f32),
+            pltpu.VMEM((BAND, BS, BS), f32),
+            pltpu.VMEM((4, 3, BS, BS), f32),
         ]
         + [dma((UNITS,))] * 8
         + [dma]
         + [dma((UNITS, 2))] * 4
         + [dma((BAND,))] * 2
         + [dma((UNITS,))] * 2
+        + [dma((BAND,)), dma((4, 3)), dma((4, 3)), dma((BAND,))]
         + [pltpu.VMEM((PER, BS, BS), f32)] * UNITS,
         compiler_params=pltpu.CompilerParams(
             collective_id=0, has_side_effects=True, vmem_limit_bytes=52 * 1024 * 1024

time: 133 us -> 97.4 us (0.73)
  the two profiles are of different devices: /device:TPU:17 before, /device:TPU:2 now
where the time goes in v2:
time: 97.4 us; the launch traced here: 97.3 us
  Pallas kernels  95.4 us (98%)
  local copies, waits for them, and re-layouts  1.63 us (2%)
    pallas_call x1, Pallas kernels, shards(): pl.pallas_call(kernel, out_shape=jax.ShapeDtypeStruct(matrix.shape, f32),...  95.4 us

profile of v2, /device:TPU:2, one launch (start us, length us, event | category | flops | bytes accessed | tf_op | source)
XLA Modules:
  0.0 97.3 jit_solution(9722862103927704759)
XLA Ops:
  0.0 0.0 copy-start
  0.0 0.7 copy-done
  0.7 0.1 select_reduce_fusion
  0.7 0.1 convert_reduce_fusion
  0.9 95.4 %shard_map.28 = f32[2048,128]{1,0:T(8,128)S(1)} custom-call(f32[16,128,128]{2,1,0:T(8,128)} %bitcast.7, s32[8,128]{1,0:T(8,128)S(1)} %pad.4.meta_s.meta_v, s32[8,128]{1,0:T(8,128)S(1)} %pad.4.meta_s.meta_v), custom_call_target="tpu_custom_call" | custom-call | tf_op jit(solution)/shard_map/pallas_call | solution.py:350
  96.3 1.0 copy.4
  (3 shorter events, 0.0 us)
Async XLA Ops:
  0.0 0.7 copy-start

commit v3 on v2

v3 whole, which is shorter than its diff:
```python
import functools

import jax
import jax.numpy as jnp
from jax import lax
from jax.experimental import pallas as pl
from jax.experimental.pallas import tpu as pltpu
from jax.sharding import PartitionSpec as P

BS = 128
PER = 7
BAND = 16
UNITS = 8
PARTS = ((0, 4), (4, 3))
LIST, SLOT, FLAG = 0, 1, 2


def index_tile(pattern):
    flags = pattern[:, 0]
    place = lax.broadcasted_iota(jnp.int32, (BAND, BAND), 0)
    upto = lax.broadcasted_iota(jnp.int32, (BAND, BAND), 1)
    count = jnp.sum(jnp.where(place <= upto, flags[:, None], 0), axis=0)
    order = lax.broadcasted_iota(jnp.int32, (BAND, BAND), 1)
    listed = jnp.sum((count[:, None] <= order).astype(jnp.int32), axis=0)
    rows = jnp.stack([jnp.minimum(listed, BAND - 1), jnp.clip(count - 1, 0, PER - 1), flags])
    return jnp.pad(rows, ((0, 8 - 3), (0, 128 - BAND)))


def split(value):
    high = value.astype(jnp.bfloat16)
    low = (value - high.astype(jnp.float32)).astype(jnp.bfloat16)
    return jnp.concatenate([high, low], axis=1)


def kernel(
    mat, meta_s, meta_v, out,
    packed, a_units, a_meta, a_idx, b_meta, b_idx, b_dense, weights,
    partial, merged, opposite, from_left, from_right, from_twin, done, passing,
    a_send, a_recv, am_send, am_recv, b_send, b_recv, bm_send, bm_recv, idx_sem, b_idx_sem,
    opp_send, opp_recv, mg_send, un_send, left_recv, right_recv, twin_send, twin_recv,
    done_send, pass_send, pass_recv, out_recv,
    *b_units,
):
    y, col, x = lax.axis_index("row"), lax.axis_index("col"), lax.axis_index("layer")
    z, q = col // 2, col % 2
    turn = 1 - 2 * q

    def at(row=None, col_=None, layer=None):
        return {
            "row": y if row is None else row,
            "col": col if col_ is None else col_,
            "layer": x if layer is None else layer,
        }

    def zdev(step):
        return at(col_=2 * ((z + step + 8) % 8) + q)

    def xdev(step):
        return at(layer=(x + step + 4) % 4)

    def ydev(step, core):
        return at(row=(y + step + 4) % 4, col_=2 * z + core)

    twin = at(col_=2 * z + 1 - q)

    barrier = pltpu.get_barrier_semaphore()

    def greet(device):
        pl.semaphore_signal(barrier, inc=1, device_id=device, device_id_type=pl.DeviceIdType.MESH)

    for device in (ydev(1, 0), ydev(1, 1), ydev(-1, 0), ydev(-1, 1)):
        greet(device)
    for step in (1, 2, 3):
        greet(xdev(step))
        greet(at(col_=2 * z + 1 - q, layer=(x + step) % 4))

    def greet_line(k, carry):
        greet(at(col_=(col + k) % BAND))
        return carry

    lax.fori_loop(1, BAND, greet_line, 0)

    for s in range(PER):
        block = mat[meta_s[LIST, s]]
        packed[s] = block
        b_units[0][s] = block.T
    own_idx = pltpu.make_async_copy(meta_v, a_idx.at[0], idx_sem)
    own_idx.start()
    own_idx.wait()

    pl.semaphore_wait(barrier, 10 + BAND - 1)

    def remote(src, dst, send, recv, device):
        return pltpu.make_async_remote_copy(
            src_ref=src, dst_ref=dst, send_sem=send, recv_sem=recv,
            device_id=device, device_id_type=pl.DeviceIdType.MESH,
        )

    def got(dst, send, recv):
        remote(dst, dst, send, recv, twin).wait_recv()

    def sent(src, send, recv):
        remote(src, src, send, recv, twin).wait_send()

    def part_of(unit, part):
        return unit.at[pl.ds(*PARTS[part])]

    def send_a(t, part, data, device):
        remote(
            part_of(data, part), part_of(a_units.at[t], part), a_send.at[t, part], a_recv.at[t, part], device
        ).start()

    def send_b(u, data, device):
        remote(data, b_units[u], b_send.at[u], b_recv.at[u], device).start()

    def a_arrive(t, part):
        got(part_of(a_units.at[t], part), a_send.at[t, part], a_recv.at[t, part])

    def a_forward(t, part):
        way = jnp.where(t % 2 == 1, turn, -turn)
        send_a(t + 2, part, a_units.at[t], zdev(way))

    def b_arrive(u):
        got(b_units[u], b_send.at[u], b_recv.at[u])

    for t in range(1, UNITS):
        step = -((t + 1) // 2) if t % 2 else t // 2
        remote(meta_v, a_meta.at[t], am_send.at[t], am_recv.at[t], zdev(-turn * step)).start()
    for u in range(1, UNITS):
        step = (0, -1, 1, -2)[u % 4]
        device = at(col_=2 * z + (q if u < 4 else 1 - q), layer=(x - turn * step + 8) % 4)
        remote(meta_v, b_meta.at[u], bm_send.at[u], bm_recv.at[u], device).start()

    def indices():
        for k in range(1, UNITS):
            got(a_meta.at[k], am_send.at[k], am_recv.at[k])
            got(b_meta.at[k], bm_send.at[k], bm_recv.at[k])
        copies = [
            pltpu.make_async_copy(a_meta.at[pl.ds(1, UNITS - 1)], a_idx.at[pl.ds(1, UNITS - 1)], idx_sem),
            pltpu.make_async_copy(b_meta.at[pl.ds(1, UNITS - 1)], b_idx.at[pl.ds(1, UNITS - 1)], b_idx_sem),
        ]
        for copy in copies:
            copy.start()
        for copy in copies:
            copy.wait()

    def b_unpack(u):
        way, core = (turn, q) if u < 4 else (-turn, 1 - q)
        group = (x + way * (0, -1, 1, -2)[u % 4] + 4) % 4

        def place(j, carry):
            slot = a_idx[0, SLOT, j] if u == 0 else b_idx[u, SLOT, j]
            flag = a_idx[0, FLAG, j] if u == 0 else b_idx[u, FLAG, j]
            b_dense[group, j, core] = split(b_units[u][slot] * flag.astype(jnp.float32))
            return carry

        lax.fori_loop(0, BAND, place, 0)

    def b_twin(u):
        send_b(4 + u, b_units[u], twin)

    def unit_row(t, way, core):
        step = jnp.where(t % 2 == 1, -((t + 1) // 2), t // 2)
        return 2 * ((z + way * step + 8) % 8) + core

    def roles(off):
        group = (x + off) % 4
        return group, (group - y + 4) % 4

    def weigh(t, load):
        for s in range(PER):
            part = split(load(s))
            weights[t, 2 * s * BS : (2 * s + 1) * BS, :] = part
            weights[t, (2 * s + 1) * BS : (2 * s + 2) * BS, :] = part

    def chunk(t, off):
        group, role = roles(off)
        i = unit_row(t, turn, q)
        places = [a_idx[t, LIST, s] for s in range(PER)]
        left = jnp.concatenate([b_dense[group, place].reshape(2 * BS, 2 * BS) for place in places], axis=1)
        both = jnp.dot(left, weights[t], preferred_element_type=jnp.float32)
        both = both[:, :BS] + both[:, BS:]
        partial[t, role, 0] = both[:BS]
        partial[t, role, 1] = both[BS:]

        @pl.when(role == 2)
        def _():
            for h, way in ((0, 1), (1, -1)):
                remote(
                    partial.at[t, 2, h], opposite.at[t, h], opp_send.at[t, h], opp_recv.at[t, h], ydev(way, q)
                ).start()

        @pl.when(role == 1)
        def _():
            remote(partial.at[t, 1, 1], from_left.at[i], un_send.at[t, 0], left_recv.at[i], ydev(1, 1)).start()

        @pl.when(role == 3)
        def _():
            remote(partial.at[t, 3, 0], from_right.at[i], un_send.at[t, 1], right_recv.at[i], ydev(-1, 0)).start()

        @pl.when(role == 0)
        def _():
            remote(partial.at[t, 0, 1 - q], from_twin.at[t], twin_send.at[t], twin_recv.at[t], twin).start()

    def merge(t, off):
        i = unit_row(t, turn, q)
        for h, mine, step, box, sem in ((0, 1, 1, from_left, left_recv), (1, 3, -1, from_right, right_recv)):
            @pl.when(roles(off)[1] == mine)
            def _():
                got(opposite.at[t, h], opp_send.at[t, h], opp_recv.at[t, h])
                merged[t, h] = opposite[t, h] + partial[t, mine, h]
                remote(merged.at[t, h], box.at[i], mg_send.at[t, h], sem.at[i], ydev(step, h)).start()

    def block_out(k):
        return out.at[pl.ds(pl.multiple_of(k * BS, BS), BS), :]

    def deliver(value, src, m, step, send):
        owner = 4 * ((x + step) % 4) + m

        @pl.when(owner == col)
        def _():
            block_out(col)[...] = value[...]

        @pl.when(owner != col)
        def _():
            remote(src, block_out(col), send, out_recv.at[col], at(col_=owner)).start()

    def relay(t, late):
        for core, way in ((q, turn), (1 - q, -turn)):
            i = unit_row(t, way, core)
            m = i // 4

            @pl.when((i % 4 == x) & (((x - y + 4) % 4 == 2) == late))
            def _():
                deliver(done.at[i], done.at[i], m, 0, done_send.at[i])

            for step in (1, 3, 2):
                @pl.when((i % 4 == x) & (((x + step - y + 4) % 4 == 2) == late))
                def _():
                    box = passing.at[m, step - 1]
                    got(box, done_send.at[i], pass_recv.at[m, step - 1])
                    deliver(box, box, m, step, pass_send.at[m, step - 1])

    def finish(t, late):
        @pl.when(((y - x + 4) % 4 == 2) == late)
        def _():
            finish_now(t)

    def finish_now(t):
        for core, way in ((q, turn), (1 - q, -turn)):
            i = unit_row(t, way, core)
            got(from_left.at[i], mg_send.at[0, 0], left_recv.at[i])
            got(from_right.at[i], mg_send.at[0, 0], right_recv.at[i])
            if core is q:
                own = partial[t, 0, q]
            else:
                got(from_twin.at[t], twin_send.at[t], twin_recv.at[t])
                own = from_twin[t]
            total = own + from_left[i] + from_right[i]
            done[i] = total
            m, step = i // 4, (x - i + 16) % 4

            @pl.when(step != 0)
            def _():
                remote(
                    done.at[i], passing.at[m, step - 1], done_send.at[i], pass_recv.at[m, step - 1], at(layer=i % 4)
                ).start()

    def each(first, stop, *steps):
        def body(t, carry):
            for step in steps:
                step(t)
            return carry

        lax.fori_loop(first, stop, body, 0)

    def chunks(*offs):
        return [functools.partial(chunk, off=off) for off in offs]

    def merges(*offs):
        return [functools.partial(merge, off=off) for off in offs]

    def finishes(late):
        return [functools.partial(finish, late=late)]

    def relays(late):
        return [functools.partial(relay, late=late)]

    def weigh_unit(t):
        weigh(t, lambda s: a_units[t, s])

    def pass_on(first, stop, part):
        each(
            first, stop, functools.partial(a_arrive, part=part), functools.partial(a_forward, part=part)
        )

    for part in range(2):
        send_a(1, part, packed, zdev(turn))
        send_a(2, part, packed, zdev(-turn))
    send_b(1, b_units[0], xdev(turn))
    send_b(2, b_units[0], xdev(-turn))
    indices()
    weigh(0, lambda s: packed[s])
    pass_on(1, 3, 0)
    b_twin(0)
    b_unpack(0)
    b_arrive(4)
    b_arrive(1)
    b_twin(1)
    send_b(3, b_units[1], xdev(turn))
    pass_on(1, 3, 1)
    b_arrive(2)
    b_unpack(4)
    each(1, 3, weigh_unit)
    chunk(0, 0)
    b_twin(2)
    b_unpack(2)
    b_unpack(1)
    each(1, 3, *chunks(0))
    b_arrive(6)
    b_unpack(6)
    b_arrive(5)
    b_unpack(5)
    each(0, 3, *chunks(1, 3))
    pass_on(3, 5, 0)
    each(1, 3, *merges(0))
    pass_on(3, 5, 1)
    merge(0, 0)
    each(0, 3, *merges(1, 3))
    b_arrive(3)
    b_twin(3)
    b_unpack(3)
    each(3, 5, weigh_unit)
    b_arrive(7)
    b_unpack(7)
    each(3, 5, *chunks(2, 0, 1, 3))
    pass_on(5, 6, 0)
    a_arrive(6, 0)
    each(0, 3, *finishes(False))
    a_arrive(6, 1)
    pass_on(5, 6, 1)
    each(3, 5, *merges(2))
    each(5, 7, weigh_unit)
    each(5, 7, *chunks(2, 0, 1, 3))
    each(3, 5, *merges(0, 1, 3))
    each(3, 5, *finishes(True))
    each(0, 3, *relays(False))
    a_arrive(7, 0)
    each(5, 7, *merges(0, 1, 3))
    each(5, 7, *merges(2))
    a_arrive(7, 1)
    each(7, 8, weigh_unit, *chunks(2, 0, 1, 3))
    each(3, 5, *relays(True))
    each(3, 5, *finishes(False))
    each(0, 3, *chunks(2))
    each(5, 7, *finishes(False))
    each(5, 7, *finishes(True))
    each(7, 8, *merges(2))
    each(3, 5, *relays(False))
    each(5, 7, *relays(True))
    each(7, 8, *merges(0, 1, 3))
    each(0, 3, *merges(2))
    each(5, 7, *relays(False))
    each(7, 8, *finishes(False))
    each(7, 8, *finishes(True))
    each(7, 8, *relays(True))
    each(0, 3, *finishes(True))
    each(7, 8, *relays(False))
    each(0, 3, *relays(True))

    for k in range(1, UNITS):
        sent(a_meta.at[k], am_send.at[k], am_recv.at[k])
        for part in range(2):
            sent(part_of(a_units.at[k], part), a_send.at[k, part], a_recv.at[k, part])
        sent(b_meta.at[k], bm_send.at[k], bm_recv.at[k])
        sent(b_units[k], b_send.at[k], b_recv.at[k])

    def drain(t, carry):
        for h in range(2):
            sent(opposite.at[t, h], opp_send.at[t, h], opp_recv.at[t, h])
            sent(merged.at[t, h], mg_send.at[t, h], opp_recv.at[t, h])
            sent(merged.at[t, h], un_send.at[t, h], opp_recv.at[t, h])
        sent(from_twin.at[t], twin_send.at[t], twin_recv.at[t])
        return carry

    lax.fori_loop(0, UNITS, drain, 0)

    def collect(k, carry):
        @pl.when((k % 4 != x) | (4 * x + k // 4 != col))
        def _():
            sent(done.at[k], done_send.at[k], out_recv.at[k])

        @pl.when(k != col)
        def _():
            got(block_out(k), done_send.at[k], out_recv.at[k])

        for step in (1, 2, 3):
            @pl.when((k < 4) & (4 * ((x + step) % 4) + k != col))
            def _():
                m = lax.rem(k, 4)
                sent(passing.at[m, step - 1], pass_send.at[m, step - 1], out_recv.at[k])

        return carry

    lax.fori_loop(0, BAND, collect, 0)


def shards(matrix, pattern):
    f32, i32 = jnp.float32, jnp.int32
    meta = index_tile(pattern)
    dma = pltpu.SemaphoreType.DMA
    return pl.pallas_call(
        kernel,
        out_shape=jax.ShapeDtypeStruct(matrix.shape, f32),
        in_specs=[
            pl.BlockSpec(memory_space=pltpu.VMEM),
            pl.BlockSpec(memory_space=pltpu.SMEM),
            pl.BlockSpec(memory_space=pltpu.VMEM),
        ],
        out_specs=pl.BlockSpec(memory_space=pltpu.VMEM),
        scratch_shapes=[
            pltpu.VMEM((PER, BS, BS), f32),
            pltpu.VMEM((UNITS, PER, BS, BS), f32),
            pltpu.VMEM((UNITS, 8, 128), i32),
            pltpu.SMEM((UNITS, 8, 128), i32),
            pltpu.VMEM((UNITS, 8, 128), i32),
            pltpu.SMEM((UNITS, 8, 128), i32),
            pltpu.VMEM((4, BAND, 2, BS, 2 * BS), jnp.bfloat16),
            pltpu.VMEM((UNITS, PER * 2 * BS, 2 * BS), jnp.bfloat16),
            pltpu.VMEM((UNITS, 4, 2, BS, BS), f32),
            pltpu.VMEM((UNITS, 2, BS, BS), f32),
            pltpu.VMEM((UNITS, 2, BS, BS), f32),
            pltpu.VMEM((BAND, BS, BS), f32),
            pltpu.VMEM((BAND, BS, BS), f32),
            pltpu.VMEM((UNITS, BS, BS), f32),
            pltpu.VMEM((BAND, BS, BS), f32),
            pltpu.VMEM((4, 3, BS, BS), f32),
        ]
        + [dma((UNITS, 2))] * 2
        + [dma((UNITS,))] * 6
        + [dma] * 2
        + [dma((UNITS, 2))] * 4
        + [dma((BAND,))] * 2
        + [dma((UNITS,))] * 2
        + [dma((BAND,)), dma((4, 3)), dma((4, 3)), dma((BAND,))]
        + [pltpu.VMEM((PER, BS, BS), f32)] * UNITS,
        compiler_params=pltpu.CompilerParams(
            collective_id=0, has_side_effects=True, vmem_limit_bytes=52 * 1024 * 1024
        ),
    )(matrix.reshape(BAND, BS, BS), meta, meta)


def solution(mesh):
    return jax.shard_map(
        shards,
        mesh=mesh,
        in_specs=(P("row", ("layer", "col")), P("row", ("layer", "col"))),
        out_specs=P("row", ("col", "layer")),
        check_vma=False,
    )
```

time: 97.4 us -> 86.5 us (0.89)
  the two profiles are of different devices: /device:TPU:2 before, /device:TPU:17 now
where the time goes in v3:
time: 86.5 us; the launch traced here: 85.8 us
  Pallas kernels  84 us (97%)
  local copies, waits for them, and re-layouts  1.63 us (2%)
    pallas_call x1, Pallas kernels, shards(): pl.pallas_call(kernel, out_shape=jax.ShapeDtypeStruct(matrix.shape, f32),...  84 us

profile of v3, /device:TPU:17, one launch (start us, length us, event | category | flops | bytes accessed | tf_op | source)
XLA Modules:
  0.0 85.8 jit_solution(5691596269250195003)
XLA Ops:
  0.0 0.0 copy-start
  0.0 0.7 copy-done
  0.7 0.1 select_reduce_fusion
  0.7 0.1 convert_reduce_fusion
  0.9 84.0 %shard_map.28 = f32[2048,128]{1,0:T(8,128)S(1)} custom-call(f32[16,128,128]{2,1,0:T(8,128)} %bitcast.7, s32[8,128]{1,0:T(8,128)S(1)} %pad.4.meta_s.meta_v, s32[8,128]{1,0:T(8,128)S(1)} %pad.4.meta_s.meta_v), custom_call_target="tpu_custom_call" | custom-call | tf_op jit(solution)/shard_map/pallas_call | solution.py:412
  84.9 1.0 %copy.4 = f32[2048,128]{1,0:T(8,128)} copy(f32[2048,128]{1,0:T(8,128)S(1)} %shard_map.28) | data formatting | bytes 2097152
  (3 shorter events, 0.0 us)
Async XLA Ops:
  0.0 0.7 copy-start

commit v4 on v3

--- a/solution.py
+++ b/solution.py
@@ -15,15 +15,13 @@
 LIST, SLOT, FLAG = 0, 1, 2
 
 
-def index_tile(pattern):
-    flags = pattern[:, 0]
-    place = lax.broadcasted_iota(jnp.int32, (BAND, BAND), 0)
-    upto = lax.broadcasted_iota(jnp.int32, (BAND, BAND), 1)
-    count = jnp.sum(jnp.where(place <= upto, flags[:, None], 0), axis=0)
-    order = lax.broadcasted_iota(jnp.int32, (BAND, BAND), 1)
-    listed = jnp.sum((count[:, None] <= order).astype(jnp.int32), axis=0)
-    rows = jnp.stack([jnp.minimum(listed, BAND - 1), jnp.clip(count - 1, 0, PER - 1), flags])
-    return jnp.pad(rows, ((0, 8 - 3), (0, 128 - BAND)))
+def index_lists(flags):
+    counts, count = [], 0
+    for flag in flags:
+        count = count + flag
+        counts.append(count)
+    listed = [jnp.minimum(sum((c <= s).astype(jnp.int32) for c in counts), BAND - 1) for s in range(PER)]
+    return listed, [jnp.clip(c - 1, 0, PER - 1) for c in counts]
 
 
 def split(value):
@@ -33,14 +31,18 @@
 
 
 def kernel(
-    mat, meta_s, meta_v, out,
-    packed, a_units, a_meta, a_idx, b_meta, b_idx, b_dense, weights,
+    pattern, matrix, out,
+    mat, own, meta_v, packed, a_units, a_meta, a_idx, b_meta, b_idx, b_dense, weights,
     partial, merged, opposite, from_left, from_right, from_twin, done, passing,
     a_send, a_recv, am_send, am_recv, b_send, b_recv, bm_send, bm_recv, idx_sem, b_idx_sem,
     opp_send, opp_recv, mg_send, un_send, left_recv, right_recv, twin_send, twin_recv,
-    done_send, pass_send, pass_recv, out_recv,
+    done_send, pass_send, pass_recv, out_recv, mat_sem,
     *b_units,
 ):
+    load = pltpu.make_async_copy(matrix, mat, mat_sem)
+    load.start()
+    flag_load = pltpu.make_async_copy(pattern, own, idx_sem)
+    flag_load.start()
     y, col, x = lax.axis_index("row"), lax.axis_index("col"), lax.axis_index("layer")
     z, q = col // 2, col % 2
     turn = 1 - 2 * q
@@ -80,8 +82,18 @@
 
     lax.fori_loop(1, BAND, greet_line, 0)
 
+    flag_load.wait()
+    flags = [own[0, j] for j in range(BAND)]
+    listed, slots = index_lists(flags)
+    row, lane = (lax.broadcasted_iota(jnp.int32, (8, 128), d) for d in (0, 1))
+    tile = jnp.zeros((8, 128), jnp.int32)
+    for kind, values in ((LIST, listed), (SLOT, slots), (FLAG, flags)):
+        for k, value in enumerate(values):
+            tile = jnp.where((row == kind) & (lane == k), value, tile)
+    meta_v[...] = tile
+    load.wait()
     for s in range(PER):
-        block = mat[meta_s[LIST, s]]
+        block = mat[listed[s]]
         packed[s] = block
         b_units[0][s] = block.T
     own_idx = pltpu.make_async_copy(meta_v, a_idx.at[0], idx_sem)
@@ -276,6 +288,13 @@
 
     def chunks(*offs):
         return [functools.partial(chunk, off=off) for off in offs]
+
+    def all_chunks(first, stop):
+        def body(n, carry):
+            chunk(n // 4, (n + 2) % 4)
+            return carry
+
+        lax.fori_loop(4 * first, 4 * stop, body, 0)
 
     def merges(*offs):
         return [functools.partial(merge, off=off) for off in offs]
@@ -333,7 +352,7 @@
     each(3, 5, weigh_unit)
     b_arrive(7)
     b_unpack(7)
-    each(3, 5, *chunks(2, 0, 1, 3))
+    all_chunks(3, 5)
     pass_on(5, 6, 0)
     a_arrive(6, 0)
     each(0, 3, *finishes(False))
@@ -341,7 +360,7 @@
     pass_on(5, 6, 1)
     each(3, 5, *merges(2))
     each(5, 7, weigh_unit)
-    each(5, 7, *chunks(2, 0, 1, 3))
+    all_chunks(5, 7)
     each(3, 5, *merges(0, 1, 3))
     each(3, 5, *finishes(True))
     each(0, 3, *relays(False))
@@ -349,7 +368,8 @@
     each(5, 7, *merges(0, 1, 3))
     each(5, 7, *merges(2))
     a_arrive(7, 1)
-    each(7, 8, weigh_unit, *chunks(2, 0, 1, 3))
+    each(7, 8, weigh_unit)
+    all_chunks(7, 8)
     each(3, 5, *relays(True))
     each(3, 5, *finishes(False))
     each(0, 3, *chunks(2))
@@ -407,18 +427,19 @@
 
 def shards(matrix, pattern):
     f32, i32 = jnp.float32, jnp.int32
-    meta = index_tile(pattern)
     dma = pltpu.SemaphoreType.DMA
     return pl.pallas_call(
         kernel,
         out_shape=jax.ShapeDtypeStruct(matrix.shape, f32),
         in_specs=[
-            pl.BlockSpec(memory_space=pltpu.VMEM),
-            pl.BlockSpec(memory_space=pltpu.SMEM),
-            pl.BlockSpec(memory_space=pltpu.VMEM),
+            pl.BlockSpec(memory_space=pl.ANY),
+            pl.BlockSpec(memory_space=pl.ANY),
         ],
         out_specs=pl.BlockSpec(memory_space=pltpu.VMEM),
         scratch_shapes=[
+            pltpu.VMEM((BAND, BS, BS), f32),
+            pltpu.SMEM((1, BAND), i32),
+            pltpu.VMEM((8, 128), i32),
             pltpu.VMEM((PER, BS, BS), f32),
             pltpu.VMEM((UNITS, PER, BS, BS), f32),
             pltpu.VMEM((UNITS, 8, 128), i32),
@@ -442,12 +463,12 @@
         + [dma((UNITS, 2))] * 4
         + [dma((BAND,))] * 2
         + [dma((UNITS,))] * 2
-        + [dma((BAND,)), dma((4, 3)), dma((4, 3)), dma((BAND,))]
+        + [dma((BAND,)), dma((4, 3)), dma((4, 3)), dma((BAND,)), dma]
         + [pltpu.VMEM((PER, BS, BS), f32)] * UNITS,
         compiler_params=pltpu.CompilerParams(
             collective_id=0, has_side_effects=True, vmem_limit_bytes=52 * 1024 * 1024
         ),
-    )(matrix.reshape(BAND, BS, BS), meta, meta)
+    )(pattern.reshape(1, BAND), matrix.reshape(BAND, BS, BS))
 
 
 def solution(mesh):

time: 86.5 us -> 85 us (0.983)
  Pallas kernels: 84 us -> 82.7 us
    pallas_call x1, Pallas kernels: 84 us -> 82.7 us  [shards(): pl.pallas_call(kernel, out_shape=jax.ShapeDtypeStruct(matrix.shape, f32),...]
where the time goes in v4:
time: 85 us; the launch traced here: 84.4 us
  Pallas kernels  82.7 us (97%)
  local copies, waits for them, and re-layouts  1.63 us (2%)
    pallas_call x1, Pallas kernels, shards(): pl.pallas_call(kernel, out_shape=jax.ShapeDtypeStruct(matrix.shape, f32),...  82.7 us

profile of v4, /device:TPU:17, one launch (start us, length us, event | category | flops | bytes accessed | tf_op | source)
XLA Modules:
  0.0 84.4 jit_solution(18412398216647936558)
XLA Ops:
  0.0 0.0 copy-start
  0.0 0.7 copy-done
  0.7 82.7 %shard_map.28 = f32[2048,128]{1,0:T(8,128)S(1)} custom-call(s32[1,16]{1,0:T(1,128)S(1)} %bitcast.2, f32[16,128,128]{2,1,0:T(8,128)} %bitcast.3), custom_call_target="tpu_custom_call" | custom-call | tf_op jit(solution)/shard_map/pallas_call | solution.py:431
  83.4 1.0 %copy.4 = f32[2048,128]{1,0:T(8,128)} copy(f32[2048,128]{1,0:T(8,128)S(1)} %shard_map.28) | data formatting | bytes 2097152
Async XLA Ops:
  0.0 0.7 copy-start

commit v5 on v4

--- a/solution.py
+++ b/solution.py
@@ -366,19 +366,19 @@
     each(0, 3, *relays(False))
     a_arrive(7, 0)
     each(5, 7, *merges(0, 1, 3))
-    each(5, 7, *merges(2))
     a_arrive(7, 1)
     each(7, 8, weigh_unit)
     all_chunks(7, 8)
+    each(5, 7, *merges(2))
     each(3, 5, *relays(True))
     each(3, 5, *finishes(False))
     each(0, 3, *chunks(2))
     each(5, 7, *finishes(False))
     each(5, 7, *finishes(True))
     each(7, 8, *merges(2))
+    each(7, 8, *merges(0, 1, 3))
     each(3, 5, *relays(False))
     each(5, 7, *relays(True))
-    each(7, 8, *merges(0, 1, 3))
     each(0, 3, *merges(2))
     each(5, 7, *relays(False))
     each(7, 8, *finishes(False))

time: 85 us -> 84.9 us (level)
  no operation moved by 1% of the time
where the time goes in v5:
time: 84.9 us; the launch traced here: 84.8 us
  Pallas kernels  83.2 us (98%)
  local copies, waits for them, and re-layouts  1.63 us (2%)
    pallas_call x1, Pallas kernels, shards(): pl.pallas_call(kernel, out_shape=jax.ShapeDtypeStruct(matrix.shape, f32),...  83.2 us

profile of v5, /device:TPU:17, one launch (start us, length us, event | category | flops | bytes accessed | tf_op | source)
XLA Modules:
  0.0 84.8 jit_solution(15477124169703985518)
XLA Ops:
  0.0 0.0 copy-start
  0.0 0.7 copy-done
  0.7 83.2 %shard_map.28 = f32[2048,128]{1,0:T(8,128)S(1)} custom-call(s32[1,16]{1,0:T(1,128)S(1)} %bitcast.2, f32[16,128,128]{2,1,0:T(8,128)} %bitcast.3), custom_call_target="tpu_custom_call" | custom-call | tf_op jit(solution)/shard_map/pallas_call | solution.py:431
  83.8 1.0 %copy.4 = f32[2048,128]{1,0:T(8,128)} copy(f32[2048,128]{1,0:T(8,128)S(1)} %shard_map.28) | data formatting | bytes 2097152
Async XLA Ops:
  0.0 0.7 copy-start

commit v6 on v5

--- a/solution.py
+++ b/solution.py
@@ -95,7 +95,6 @@
     for s in range(PER):
         block = mat[listed[s]]
         packed[s] = block
-        b_units[0][s] = block.T
     own_idx = pltpu.make_async_copy(meta_v, a_idx.at[0], idx_sem)
     own_idx.start()
     own_idx.wait()
@@ -316,6 +315,8 @@
     for part in range(2):
         send_a(1, part, packed, zdev(turn))
         send_a(2, part, packed, zdev(-turn))
+    for s in range(PER):
+        b_units[0][s] = packed[s].T
     send_b(1, b_units[0], xdev(turn))
     send_b(2, b_units[0], xdev(-turn))
     indices()

time: 84.9 us -> 84.9 us (level)
  no operation moved by 1% of the time
where the time goes in v6:
time: 84.9 us; the launch traced here: 84.8 us
  Pallas kernels  83.2 us (98%)
  local copies, waits for them, and re-layouts  1.63 us (2%)
    pallas_call x1, Pallas kernels, shards(): pl.pallas_call(kernel, out_shape=jax.ShapeDtypeStruct(matrix.shape, f32),...  83.2 us

profile of v6, /device:TPU:17, one launch (start us, length us, event | category | flops | bytes accessed | tf_op | source)
XLA Modules:
  0.0 84.8 jit_solution(16827817784645607446)
XLA Ops:
  0.0 0.0 copy-start
  0.0 0.7 copy-done
  0.7 83.2 %shard_map.28 = f32[2048,128]{1,0:T(8,128)S(1)} custom-call(s32[1,16]{1,0:T(1,128)S(1)} %bitcast.2, f32[16,128,128]{2,1,0:T(8,128)} %bitcast.3), custom_call_target="tpu_custom_call" | custom-call | tf_op jit(solution)/shard_map/pallas_call | solution.py:432
  83.8 1.0 %copy.4 = f32[2048,128]{1,0:T(8,128)} copy(f32[2048,128]{1,0:T(8,128)S(1)} %shard_map.28) | data formatting | bytes 2097152
Async XLA Ops:
  0.0 0.7 copy-start
